TPU v7x, 256 devices: a whole 4x4x8 slice. The times are simulated.
256 devices in a mesh: ctx: 32 (over z, x), head: 8 (over y, core).
Axes of the slice: x: 4, y: 4, z: 8, core: 2. Of those that a mesh axis runs over, the one named last changes fastest.
Arguments:
- queries: bfloat16 [8192, 4096], P('ctx', 'head'), may hold values from -6 to 6
- keys: bfloat16 [8192, 4096], P('ctx', 'head'), may hold values from -6 to 6
- values: bfloat16 [8192, 4096], P('ctx', 'head'), may hold values from -6 to 6
- tan_queries: bfloat16 [8192, 4096], P('ctx', 'head'), may hold values from -6 to 6
- tan_keys: bfloat16 [8192, 4096], P('ctx', 'head'), may hold values from -6 to 6
- tan_values: bfloat16 [8192, 4096], P('ctx', 'head'), may hold values from -6 to 6
- w_out: bfloat16 [4096, 4096], P('head'), may hold values from -0.125 to 0.125
Outputs:
- mixed: bfloat16 [4096, 8192], P('head', 'ctx')
- tangent_mixed: bfloat16 [4096, 8192], P('head', 'ctx')
All inputs are finite; a program needn't handle non-finite values.
Results may differ from a plain program's by a relative error of at most 0.022.
Values may be sent and summed in bfloat16 or wider, within the bound.
No kernel may reach another device: no remote copies, remote signals or barrier semaphores. Data moves between devices by JAX's collectives and lax.ppermute only.
A program may use at most 128 MiB of HBM per device.

v0:
```python
import math

import jax
import jax.numpy as jnp
from jax import lax
from jax.sharding import PartitionSpec as P

HD = 128
BLOCK = 128


MASKED_SCORE = -1e30
LOG_TWO = math.log(2.0)


def as_sent(shard):
    return jax.tree.map(lambda a: a.astype(jnp.bfloat16) if a.dtype == jnp.float32 else a, shard)


def partner(block, axis, bit):
    count = lax.axis_size(axis)
    route = []
    for low in range(count):
        high = low | 1 << bit
        if high != low and high < count:
            route += [(low, high), (high, low)]
    return lax.ppermute(block, axis, route)


def pool_pairs(array):
    row_count = array.shape[-2]
    paired = array.astype(jnp.float32).reshape(
        array.shape[:-2] + (row_count // 2, 2, array.shape[-1])
    )
    return (0.5 * (paired[..., 0, :] + paired[..., 1, :])).astype(jnp.bfloat16)


def level_terms(queries, keys, values, tan_q, tan_k, tan_v, offset, allowed):
    scale = 1.0 / math.sqrt(queries.shape[-1])
    form = "...qd,...kd->...qk"
    scores = jnp.einsum(form, queries, keys, preferred_element_type=jnp.float32) * scale + offset
    slopes = (
        jnp.einsum(form, tan_q, keys, preferred_element_type=jnp.float32)
        + jnp.einsum(form, queries, tan_k, preferred_element_type=jnp.float32)
    ) * scale
    if allowed is not None:
        scores = jnp.where(allowed, scores, MASKED_SCORE)
    top = jnp.max(scores, axis=-1)
    probs = jnp.exp(scores - top[..., None])
    moved32 = probs * slopes
    weights = probs.astype(jnp.bfloat16)
    moved = moved32.astype(jnp.bfloat16)
    mixing = "...qk,...kd->...qd"
    num = jnp.einsum(mixing, weights, values, preferred_element_type=jnp.float32)
    acc = jnp.einsum(mixing, moved, values, preferred_element_type=jnp.float32) + jnp.einsum(
        mixing, weights, tan_v, preferred_element_type=jnp.float32
    )
    return (top, jnp.sum(probs, axis=-1), num, acc, jnp.sum(moved32, axis=-1))


def flatten(stats, lead, row_count, width):
    top, den, num, acc, curv = stats
    flat = lead + (row_count,)
    return (
        top.reshape(flat),
        den.reshape(flat),
        num.reshape(flat + (width,)),
        acc.reshape(flat + (width,)),
        curv.reshape(flat),
    )


def leaf_terms(queries, keys, values, tan_q, tan_k, tan_v):
    lead = queries.shape[:-2]
    row_count = queries.shape[-2]
    width = queries.shape[-1]
    block_count = row_count // BLOCK

    def blocks(array):
        return array.reshape(lead + (block_count, BLOCK, width))

    def widen(array):
        tiled = blocks(array)
        return jnp.concatenate([jnp.roll(tiled, 1, axis=-3), tiled], axis=-2)

    odd_blocks = jnp.arange(block_count) % 2 == 1
    earlier = jnp.broadcast_to(odd_blocks[:, None, None], (block_count, BLOCK, BLOCK))
    causal = jnp.broadcast_to(
        jnp.arange(BLOCK)[:, None] >= jnp.arange(BLOCK)[None, :], (block_count, BLOCK, BLOCK)
    )
    allowed = jnp.concatenate([earlier, causal], axis=-1)
    stats = level_terms(
        blocks(queries),
        widen(keys),
        widen(values),
        blocks(tan_q),
        widen(tan_k),
        widen(tan_v),
        0.0,
        allowed,
    )
    return flatten(stats, lead, row_count, width)


def remote_terms(query_side, others, level_num, active):
    stats = level_terms(
        query_side[0],
        others[0],
        others[1],
        query_side[1],
        others[2],
        others[3],
        level_num * LOG_TWO,
        None,
    )
    return (jnp.where(active, stats[0], MASKED_SCORE),) + stats[1:]


def expand(stats, factor):
    top, den, num, acc, curv = stats
    return (
        jnp.repeat(top, factor, axis=-1),
        jnp.repeat(den, factor, axis=-1),
        jnp.repeat(num, factor, axis=-2),
        jnp.repeat(acc, factor, axis=-2),
        jnp.repeat(curv, factor, axis=-1),
    )


def merge(carry, stats):
    top_old, den_old, num_old, acc_old, curv_old = carry
    top_new, den_new, num_new, acc_new, curv_new = stats
    top = jnp.maximum(top_old, top_new)
    keep_old = jnp.exp(top_old - top)
    keep_new = jnp.exp(top_new - top)
    return (
        top,
        keep_old * den_old + keep_new * den_new,
        keep_old[..., None] * num_old + keep_new[..., None] * num_new,
        keep_old[..., None] * acc_old + keep_new[..., None] * acc_new,
        keep_old * curv_old + keep_new * curv_new,
    )


def finish(carry):
    top, den, num, acc, curv = carry
    attended = num / den[..., None]
    attended_tan = (acc - attended * curv[..., None]) / den[..., None]
    return (attended.astype(jnp.bfloat16), attended_tan.astype(jnp.bfloat16))


def on_device(queries, keys, values, tan_queries, tan_keys, tan_values, w_out):
    row_count = queries.shape[0]
    heads_here = queries.shape[1] // HD

    def split_heads(array):
        return array.reshape(row_count, heads_here, HD).transpose(1, 0, 2)

    arrays = tuple(
        (split_heads(array) for array in (queries, keys, values, tan_queries, tan_keys, tan_values))
    )
    local_levels = (row_count // BLOCK).bit_length() - 1
    carry = leaf_terms(*arrays)
    current = arrays
    level_num = 1
    current = tuple((pool_pairs(array) for array in current))
    query_side = (current[0], current[3])
    owned = (current[1], current[2], current[4], current[5])
    position = lax.axis_index("ctx")
    bit_count = lax.axis_size("ctx").bit_length() - 1
    for bit_index in range(bit_count):
        others = jax.tree.map(
            lambda part, own: part.astype(own.dtype),
            partner(as_sent(owned), "ctx", bit_index),
            owned,
        )
        active = position >> bit_index & 1 == 1
        level_num = local_levels + bit_index
        carry = merge(
            carry, expand(remote_terms(query_side, others, level_num, active), 2**level_num)
        )
        if bit_index + 1 < bit_count:
            owned = tuple(
                (
                    pool_pairs(
                        jnp.where(
                            active,
                            jnp.concatenate([theirs, mine], axis=1),
                            jnp.concatenate([mine, theirs], axis=1),
                        )
                    )
                    for mine, theirs in zip(owned, others)
                )
            )
            query_side = tuple((pool_pairs(array) for array in query_side))
    attended, attended_tan = finish(carry)

    def join_heads(array):
        return array.transpose(1, 0, 2).reshape(row_count, heads_here * HD)

    stacked = jnp.concatenate([join_heads(attended), join_heads(attended_tan)], axis=0)
    summed = lax.psum_scatter(
        lax.dot_general(
            w_out, stacked, (((0,), (1,)), ((), ())), preferred_element_type=jnp.float32
        ).astype(jnp.bfloat16),
        "head",
        scatter_dimension=0,
        tiled=True,
    )
    return (summed[:, :row_count], summed[:, row_count:])


def solution(mesh):
    placed = (
        P("ctx", "head"),
        P("ctx", "head"),
        P("ctx", "head"),
        P("ctx", "head"),
        P("ctx", "head"),
        P("ctx", "head"),
        P("head", None),
    )
    return jax.shard_map(
        on_device,
        mesh=mesh,
        in_specs=placed,
        out_specs=(P("head", "ctx"), P("head", "ctx")),
        check_vma=False,
    )
```

profile of v0, /device:TPU:1, one launch (start us, length us, event | category | flops | bytes accessed | tf_op | source)
XLA Modules:
  0.0 188.0 jit_solution(10374976876116783808)
XLA Ops:
  7.2 1.1 copy.335
  9.6 2.0 %collective-permute-start = (bf16[4,128,128]{2,1,0:T(8,128)(2,1)}, bf16[4,128,128]{2,1,0:T(8,128)(2,1)S(1)}, u32[]{:S(2)}, u32[]{:S(2)}) collective-permute-start(bf16[4,128,128]{2,1,0:T(8,128)(2,1)} %fusion.66), channel_id=1, source_target_pairs={{0,8},{8,0},{16,24},{24,16},{32,40},{40,32},{48,56},{56,48},{64,72... | collective-permute-start | bytes 393224 | tf_op jit(solution)/shard_map/ppermute | solution.py:27
  15.4 1.5 collective-permute-start.10
  23.4 1.6 fusion.197
  31.3 1.2 maximum_select_fusion
  33.0 3.3 %collective-permute-start.1 = (bf16[4,128,128]{2,1,0:T(8,128)(2,1)S(1)}, bf16[4,128,128]{2,1,0:T(8,128)(2,1)S(1)}, u32[]{:S(2)}, u32[]{:S(2)}) collective-permute-start(bf16[4,128,128]{2,1,0:T(8,128)(2,1)S(1)} %fusion.67), channel_id=1, source_target_pairs={{0,16},{16,0},{8,24},{24,8},{32,48},{48,32},{40,56},{56,40},{64,80... | collective-permute-start | bytes 393224 | tf_op jit(solution)/shard_map/ppermute | solution.py:27
  36.3 1.4 maximum_select_fusion.8
  39.2 3.0 %collective-permute-start.12 = (bf16[4,128,128]{2,1,0:T(8,128)(2,1)S(1)}, bf16[4,128,128]{2,1,0:T(8,128)(2,1)}, u32[]{:S(2)}, u32[]{:S(2)}) collective-permute-start(bf16[4,128,128]{2,1,0:T(8,128)(2,1)S(1)} %fusion.78), channel_id=1, source_target_pairs={{0,16},{16,0},{8,24},{24,8},{32,48},{48,32},{40,56},{56,40},{64,80... | collective-permute-start | bytes 393224 | tf_op jit(solution)/shard_map/ppermute | solution.py:27
  43.3 1.1 fusion.87
  46.3 1.1 fusion.104
  48.5 1.9 %collective-permute-start.2 = (bf16[4,128,128]{2,1,0:T(8,128)(2,1)S(1)}, bf16[4,128,128]{2,1,0:T(8,128)(2,1)S(1)}, u32[]{:S(2)}, u32[]{:S(2)}) collective-permute-start(bf16[4,128,128]{2,1,0:T(8,128)(2,1)S(1)} %fusion.68), channel_id=1, source_target_pairs={{0,32},{32,0},{8,40},{40,8},{16,48},{48,16},{24,56},{56,24},{64,96... | collective-permute-start | bytes 393224 | tf_op jit(solution)/shard_map/ppermute | solution.py:27
  53.4 1.5 collective-permute-start.14
  61.4 3.1 %collective-permute-start.17 = (bf16[4,128,128]{2,1,0:T(8,128)(2,1)S(1)}, bf16[4,128,128]{2,1,0:T(8,128)(2,1)}, u32[]{:S(2)}, u32[]{:S(2)}) collective-permute-start(bf16[4,128,128]{2,1,0:T(8,128)(2,1)S(1)} %fusion.83), channel_id=1, source_target_pairs={{0,64},{64,0},{8,72},{72,8},{16,80},{80,16},{24,88},{88,24},{32,96... | collective-permute-start | bytes 393224 | tf_op jit(solution)/shard_map/ppermute | solution.py:27
  65.8 2.4 %collective-permute-start.8 = (bf16[4,128,128]{2,1,0:T(8,128)(2,1)S(1)}, bf16[4,128,128]{2,1,0:T(8,128)(2,1)S(1)}, u32[]{:S(2)}, u32[]{:S(2)}) collective-permute-start(bf16[4,128,128]{2,1,0:T(8,128)(2,1)S(1)} %fusion.74), channel_id=1, source_target_pairs={{0,64},{64,0},{8,72},{72,8},{16,80},{80,16},{24,88},{88,24},{32,96... | collective-permute-start | bytes 393224 | tf_op jit(solution)/shard_map/ppermute | solution.py:27
  71.5 1.1 fusion.144
  76.4 6.0 %collective-permute-start.19 = (bf16[4,128,128]{2,1,0:T(8,128)(2,1)}, bf16[4,128,128]{2,1,0:T(8,128)(2,1)}, u32[]{:S(2)}, u32[]{:S(2)}) collective-permute-start(bf16[4,128,128]{2,1,0:T(8,128)(2,1)} %fusion.85), channel_id=1, source_target_pairs={{0,128},{128,0},{8,136},{136,8},{16,144},{144,16},{24,152},{152,24... | collective-permute-start | bytes 393224 | tf_op jit(solution)/shard_map/ppermute | solution.py:27
  83.0 4.9 %collective-permute-start.4 = (bf16[4,128,128]{2,1,0:T(8,128)(2,1)S(1)}, bf16[4,128,128]{2,1,0:T(8,128)(2,1)S(1)}, u32[]{:S(2)}, u32[]{:S(2)}) collective-permute-start(bf16[4,128,128]{2,1,0:T(8,128)(2,1)S(1)} %fusion.70), channel_id=1, source_target_pairs={{0,128},{128,0},{8,136},{136,8},{16,144},{144,16},{24,152},{152,24... | collective-permute-start | bytes 393224 | tf_op jit(solution)/shard_map/ppermute | solution.py:27
  88.4 2.3 %collective-permute-start.9 = (bf16[4,128,128]{2,1,0:T(8,128)(2,1)S(1)}, bf16[4,128,128]{2,1,0:T(8,128)(2,1)S(1)}, u32[]{:S(2)}, u32[]{:S(2)}) collective-permute-start(bf16[4,128,128]{2,1,0:T(8,128)(2,1)S(1)} %fusion.75), channel_id=1, source_target_pairs={{0,128},{128,0},{8,136},{136,8},{16,144},{144,16},{24,152},{152,24... | collective-permute-start | bytes 393224 | tf_op jit(solution)/shard_map/ppermute | solution.py:27
  91.2 25.1 %collective-permute-start.18 = (bf16[4,128,128]{2,1,0:T(8,128)(2,1)S(1)}, bf16[4,128,128]{2,1,0:T(8,128)(2,1)S(1)}, u32[]{:S(2)}, u32[]{:S(2)}) collective-permute-start(bf16[4,128,128]{2,1,0:T(8,128)(2,1)S(1)} %fusion.84), channel_id=1, source_target_pairs={{0,128},{128,0},{8,136},{136,8},{16,144},{144,16},{24,152},{152,24... | collective-permute-start | bytes 393224 | tf_op jit(solution)/shard_map/ppermute | solution.py:27
  119.2 1.1 fusion.171
  127.1 1.9 %convert_bitcast_fusion = (bf16[256,4,128]{2,0,1:T(8,128)(2,1)S(1)}, f32[4,256,128]{2,1,0:T(8,128)S(1)}) fusion(f32[4,256]{1,0:T(4,128)S(1)} %fusion.169, f32[4,8,128]{2,1,0:T(8,128)S(1)} %fusion.179, f32[4,256]{1,0:T(4,128)S(1)} %get-tuple-element.19, f32[4,16,128]{2,1,0:T(8,128)S(1)} %fusion.173, f32[4,256]{1,0:T(4,128)S(1)} %get-tuple-element.18, ...), kind=kLoop, calls=%fused_computation.117 | loop fusion | flops 2228224 | bytes 2519040 | tf_op jit(solution)/shard_map/transpose | solution.py:199
  130.5 2.0 %fusion.59 = bf16[4,256,128]{2,1,0:T(8,128)(2,1)S(1)} fusion(f32[4,256,128]{2,1,0:T(8,128)S(1)} %get-tuple-element.13, f32[4,256,128]{2,1,0:T(8,128)S(1)} %bitcast.455, f32[4,256,128]{2,1,0:T(8,128)S(1)} %bitcast.457, f32[4,2,128,128]{3,2,1,0:T(8,128)S(1)} %convolution_add_fusion.1, f32[4,256]{1,0:T(4,128)S(1)} %get-tuple-element.14, ...), kind=kLoop, calls=%fused_computation.89 | loop fusion | flops 2490368 | bytes 2523136 | tf_op jit(solution)/shard_map/convert_element_type | solution.py:149
  132.9 6.5 %fusion = bf16[4096,512]{0,1:T(8,128)(2,1)} fusion(bf16[512,4096]{1,0:T(8,128)(2,1)} %param.13, bf16[256,512]{0,1:T(8,128)(2,1)S(1)} %bitcast.469, bf16[256,512]{0,1:T(8,128)(2,1)S(1)} %bitcast.470), kind=kOutput, calls=%fused_computation.1 | convolution fusion | flops 2150629376 | bytes 8912896 | tf_op jit(solution)/shard_map/dot_general | solution.py:203
  139.4 39.0 %reduce-scatter.2.cloned.1.call-done = bf16[512,512]{0,1:T(8,128)(2,1)} async-done(((bf16[4096,512]{0,1:T(8,128)(2,1)}), bf16[512,512]{0,1:T(8,128)(2,1)}) %reduce-scatter.2.cloned.1.call-update) | async-done | bytes 524304 | tf_op jit(solution)/shard_map/reduce_scatter | solution.py:202
  (227 shorter events, 56.6 us)
Async XLA Ops:
  7.2 171.3 %reduce-scatter.2.cloned.1.call-start = ((), (), s32[]{:S(2)}) async-start(), calls=%async_computation.1 | async-start | bytes 4718592 | tf_op jit(solution)/shard_map/reduce_scatter | solution.py:202
  9.6 21.7 %collective-permute-start = (bf16[4,128,128]{2,1,0:T(8,128)(2,1)}, bf16[4,128,128]{2,1,0:T(8,128)(2,1)S(1)}, u32[]{:S(2)}, u32[]{:S(2)}) collective-permute-start(bf16[4,128,128]{2,1,0:T(8,128)(2,1)} %fusion.66), channel_id=1, source_target_pairs={{0,8},{8,0},{16,24},{24,16},{32,40},{40,32},{48,56},{56,48},{64,72... | collective-permute-start | bytes 393224 | tf_op jit(solution)/shard_map/ppermute | solution.py:27
  14.0 17.3 %collective-permute-start.5 = (bf16[4,128,128]{2,1,0:T(8,128)(2,1)}, bf16[4,128,128]{2,1,0:T(8,128)(2,1)S(1)}, u32[]{:S(2)}, u32[]{:S(2)}) collective-permute-start(bf16[4,128,128]{2,1,0:T(8,128)(2,1)} %fusion.71), channel_id=1, source_target_pairs={{0,8},{8,0},{16,24},{24,16},{32,40},{40,32},{48,56},{56,48},{64,72... | collective-permute-start | bytes 393224 | tf_op jit(solution)/shard_map/ppermute | solution.py:27
  15.4 20.9 %collective-permute-start.10 = (bf16[4,128,128]{2,1,0:T(8,128)(2,1)}, bf16[4,128,128]{2,1,0:T(8,128)(2,1)}, u32[]{:S(2)}, u32[]{:S(2)}) collective-permute-start(bf16[4,128,128]{2,1,0:T(8,128)(2,1)} %fusion.76), channel_id=1, source_target_pairs={{0,8},{8,0},{16,24},{24,16},{32,40},{40,32},{48,56},{56,48},{64,72... | collective-permute-start | bytes 393224 | tf_op jit(solution)/shard_map/ppermute | solution.py:27
  18.3 18.0 %collective-permute-start.11 = (bf16[4,128,128]{2,1,0:T(8,128)(2,1)}, bf16[4,128,128]{2,1,0:T(8,128)(2,1)}, u32[]{:S(2)}, u32[]{:S(2)}) collective-permute-start(bf16[4,128,128]{2,1,0:T(8,128)(2,1)} %fusion.77), channel_id=1, source_target_pairs={{0,8},{8,0},{16,24},{24,16},{32,40},{40,32},{48,56},{56,48},{64,72... | collective-permute-start | bytes 393224 | tf_op jit(solution)/shard_map/ppermute | solution.py:27
  33.0 15.0 %collective-permute-start.1 = (bf16[4,128,128]{2,1,0:T(8,128)(2,1)S(1)}, bf16[4,128,128]{2,1,0:T(8,128)(2,1)S(1)}, u32[]{:S(2)}, u32[]{:S(2)}) collective-permute-start(bf16[4,128,128]{2,1,0:T(8,128)(2,1)S(1)} %fusion.67), channel_id=1, source_target_pairs={{0,16},{16,0},{8,24},{24,8},{32,48},{48,32},{40,56},{56,40},{64,80... | collective-permute-start | bytes 393224 | tf_op jit(solution)/shard_map/ppermute | solution.py:27
  38.7 11.6 %collective-permute-start.13 = (bf16[4,128,128]{2,1,0:T(8,128)(2,1)}, bf16[4,128,128]{2,1,0:T(8,128)(2,1)S(1)}, u32[]{:S(2)}, u32[]{:S(2)}) collective-permute-start(bf16[4,128,128]{2,1,0:T(8,128)(2,1)} %fusion.79), channel_id=1, source_target_pairs={{0,16},{16,0},{8,24},{24,8},{32,48},{48,32},{40,56},{56,40},{64,80... | collective-permute-start | bytes 393224 | tf_op jit(solution)/shard_map/ppermute | solution.py:27
  39.2 12.8 %collective-permute-start.12 = (bf16[4,128,128]{2,1,0:T(8,128)(2,1)S(1)}, bf16[4,128,128]{2,1,0:T(8,128)(2,1)}, u32[]{:S(2)}, u32[]{:S(2)}) collective-permute-start(bf16[4,128,128]{2,1,0:T(8,128)(2,1)S(1)} %fusion.78), channel_id=1, source_target_pairs={{0,16},{16,0},{8,24},{24,8},{32,48},{48,32},{40,56},{56,40},{64,80... | collective-permute-start | bytes 393224 | tf_op jit(solution)/shard_map/ppermute | solution.py:27
  42.6 12.3 %collective-permute-start.6 = (bf16[4,128,128]{2,1,0:T(8,128)(2,1)S(1)}, bf16[4,128,128]{2,1,0:T(8,128)(2,1)S(1)}, u32[]{:S(2)}, u32[]{:S(2)}) collective-permute-start(bf16[4,128,128]{2,1,0:T(8,128)(2,1)S(1)} %fusion.72), channel_id=1, source_target_pairs={{0,16},{16,0},{8,24},{24,8},{32,48},{48,32},{40,56},{56,40},{64,80... | collective-permute-start | bytes 393224 | tf_op jit(solution)/shard_map/ppermute | solution.py:27
  48.5 16.0 %collective-permute-start.2 = (bf16[4,128,128]{2,1,0:T(8,128)(2,1)S(1)}, bf16[4,128,128]{2,1,0:T(8,128)(2,1)S(1)}, u32[]{:S(2)}, u32[]{:S(2)}) collective-permute-start(bf16[4,128,128]{2,1,0:T(8,128)(2,1)S(1)} %fusion.68), channel_id=1, source_target_pairs={{0,32},{32,0},{8,40},{40,8},{16,48},{48,16},{24,56},{56,24},{64,96... | collective-permute-start | bytes 393224 | tf_op jit(solution)/shard_map/ppermute | solution.py:27
  51.8 8.1 %collective-permute-start.15 = (bf16[4,128,128]{2,1,0:T(8,128)(2,1)S(1)}, bf16[4,128,128]{2,1,0:T(8,128)(2,1)}, u32[]{:S(2)}, u32[]{:S(2)}) collective-permute-start(bf16[4,128,128]{2,1,0:T(8,128)(2,1)S(1)} %fusion.81), channel_id=1, source_target_pairs={{0,32},{32,0},{8,40},{40,8},{16,48},{48,16},{24,56},{56,24},{64,96... | collective-permute-start | bytes 393224 | tf_op jit(solution)/shard_map/ppermute | solution.py:27
  53.4 14.9 %collective-permute-start.14 = (bf16[4,128,128]{2,1,0:T(8,128)(2,1)S(1)}, bf16[4,128,128]{2,1,0:T(8,128)(2,1)S(1)}, u32[]{:S(2)}, u32[]{:S(2)}) collective-permute-start(bf16[4,128,128]{2,1,0:T(8,128)(2,1)S(1)} %fusion.80), channel_id=1, source_target_pairs={{0,32},{32,0},{8,40},{40,8},{16,48},{48,16},{24,56},{56,24},{64,96... | collective-permute-start | bytes 393224 | tf_op jit(solution)/shard_map/ppermute | solution.py:27
  55.4 9.9 %collective-permute-start.7 = (bf16[4,128,128]{2,1,0:T(8,128)(2,1)S(1)}, bf16[4,128,128]{2,1,0:T(8,128)(2,1)S(1)}, u32[]{:S(2)}, u32[]{:S(2)}) collective-permute-start(bf16[4,128,128]{2,1,0:T(8,128)(2,1)S(1)} %fusion.73), channel_id=1, source_target_pairs={{0,32},{32,0},{8,40},{40,8},{16,48},{48,16},{24,56},{56,24},{64,96... | collective-permute-start | bytes 393224 | tf_op jit(solution)/shard_map/ppermute | solution.py:27
  61.4 8.9 %copy-start.6 = (bf16[4,32,1,128]{3,2,1,0:T(2,128)(2,1)S(1)}, bf16[4,32,1,128]{3,2,1,0:T(2,128)(2,1)}, u32[]{:S(2)}) copy-start(bf16[4,32,1,128]{3,2,1,0:T(2,128)(2,1)} %get-tuple-element.28) | copy-start | bytes 98308
  61.4 12.9 %collective-permute-start.17 = (bf16[4,128,128]{2,1,0:T(8,128)(2,1)S(1)}, bf16[4,128,128]{2,1,0:T(8,128)(2,1)}, u32[]{:S(2)}, u32[]{:S(2)}) collective-permute-start(bf16[4,128,128]{2,1,0:T(8,128)(2,1)S(1)} %fusion.83), channel_id=1, source_target_pairs={{0,64},{64,0},{8,72},{72,8},{16,80},{80,16},{24,88},{88,24},{32,96... | collective-permute-start | bytes 393224 | tf_op jit(solution)/shard_map/ppermute | solution.py:27
  65.0 17.5 %collective-permute-start.3 = (bf16[4,128,128]{2,1,0:T(8,128)(2,1)S(1)}, bf16[4,128,128]{2,1,0:T(8,128)(2,1)S(1)}, u32[]{:S(2)}, u32[]{:S(2)}) collective-permute-start(bf16[4,128,128]{2,1,0:T(8,128)(2,1)S(1)} %fusion.69), channel_id=1, source_target_pairs={{0,64},{64,0},{8,72},{72,8},{16,80},{80,16},{24,88},{88,24},{32,96... | collective-permute-start | bytes 393224 | tf_op jit(solution)/shard_map/ppermute | solution.py:27
  65.8 22.1 %collective-permute-start.8 = (bf16[4,128,128]{2,1,0:T(8,128)(2,1)S(1)}, bf16[4,128,128]{2,1,0:T(8,128)(2,1)S(1)}, u32[]{:S(2)}, u32[]{:S(2)}) collective-permute-start(bf16[4,128,128]{2,1,0:T(8,128)(2,1)S(1)} %fusion.74), channel_id=1, source_target_pairs={{0,64},{64,0},{8,72},{72,8},{16,80},{80,16},{24,88},{88,24},{32,96... | collective-permute-start | bytes 393224 | tf_op jit(solution)/shard_map/ppermute | solution.py:27
  68.8 21.9 %collective-permute-start.16 = (bf16[4,128,128]{2,1,0:T(8,128)(2,1)S(1)}, bf16[4,128,128]{2,1,0:T(8,128)(2,1)S(1)}, u32[]{:S(2)}, u32[]{:S(2)}) collective-permute-start(bf16[4,128,128]{2,1,0:T(8,128)(2,1)S(1)} %fusion.82), channel_id=1, source_target_pairs={{0,64},{64,0},{8,72},{72,8},{16,80},{80,16},{24,88},{88,24},{32,96... | collective-permute-start | bytes 393224 | tf_op jit(solution)/shard_map/ppermute | solution.py:27
  75.3 40.9 %copy-start.7 = (bf16[4,16,1,128]{3,2,1,0:T(2,128)(2,1)S(1)}, bf16[4,16,1,128]{3,2,1,0:T(2,128)(2,1)}, u32[]{:S(2)}) copy-start(bf16[4,16,1,128]{3,2,1,0:T(2,128)(2,1)} %get-tuple-element.32) | copy-start | bytes 49156
  76.4 52.6 %collective-permute-start.19 = (bf16[4,128,128]{2,1,0:T(8,128)(2,1)}, bf16[4,128,128]{2,1,0:T(8,128)(2,1)}, u32[]{:S(2)}, u32[]{:S(2)}) collective-permute-start(bf16[4,128,128]{2,1,0:T(8,128)(2,1)} %fusion.85), channel_id=1, source_target_pairs={{0,128},{128,0},{8,136},{136,8},{16,144},{144,16},{24,152},{152,24... | collective-permute-start | bytes 393224 | tf_op jit(solution)/shard_map/ppermute | solution.py:27
  82.9 44.1 %copy-start.5 = (f32[4,32,128]{2,1,0:T(8,128)S(1)}, f32[4,32,128]{2,1,0:T(8,128)}, u32[]{:S(2)}) copy-start(f32[4,32,128]{2,1,0:T(8,128)} %fusion.146) | copy-start | bytes 196612
  83.0 37.7 %collective-permute-start.4 = (bf16[4,128,128]{2,1,0:T(8,128)(2,1)S(1)}, bf16[4,128,128]{2,1,0:T(8,128)(2,1)S(1)}, u32[]{:S(2)}, u32[]{:S(2)}) collective-permute-start(bf16[4,128,128]{2,1,0:T(8,128)(2,1)S(1)} %fusion.70), channel_id=1, source_target_pairs={{0,128},{128,0},{8,136},{136,8},{16,144},{144,16},{24,152},{152,24... | collective-permute-start | bytes 393224 | tf_op jit(solution)/shard_map/ppermute | solution.py:27
  88.4 37.5 %collective-permute-start.9 = (bf16[4,128,128]{2,1,0:T(8,128)(2,1)S(1)}, bf16[4,128,128]{2,1,0:T(8,128)(2,1)S(1)}, u32[]{:S(2)}, u32[]{:S(2)}) collective-permute-start(bf16[4,128,128]{2,1,0:T(8,128)(2,1)S(1)} %fusion.75), channel_id=1, source_target_pairs={{0,128},{128,0},{8,136},{136,8},{16,144},{144,16},{24,152},{152,24... | collective-permute-start | bytes 393224 | tf_op jit(solution)/shard_map/ppermute | solution.py:27
  91.2 31.8 %collective-permute-start.18 = (bf16[4,128,128]{2,1,0:T(8,128)(2,1)S(1)}, bf16[4,128,128]{2,1,0:T(8,128)(2,1)S(1)}, u32[]{:S(2)}, u32[]{:S(2)}) collective-permute-start(bf16[4,128,128]{2,1,0:T(8,128)(2,1)S(1)} %fusion.84), channel_id=1, source_target_pairs={{0,128},{128,0},{8,136},{136,8},{16,144},{144,16},{24,152},{152,24... | collective-permute-start | bytes 393224 | tf_op jit(solution)/shard_map/ppermute | solution.py:27
  (5 other events, 34.3 us)
Sparse Core Ops, SparseCore 0:
  139.6 38.8 reduce-scatter.1
where the time goes:
time: 191 us; the launch traced here: 188 us
  starting transfers between devices  57.9 us (30%)
  waiting for transfers between devices  40.1 us (21%)
  other arithmetic  25.5 us (13%)
  matrix products  25.5 us (13%)
  local copies, waits for them, and re-layouts  24 us (13%)
  between operations  15 us (8%)
    ppermute x20, starting transfers between devices, partner(): return lax.ppermute(block, axis, route)  57.9 us
    reduce_scatter x1, waiting for transfers between devices, on_device(): lax.psum_scatter(lax.dot_general(w_out, stacked, (((0,), (1,)), ((), ()))...  39 us
    slice x24, local copies, waits for them, and re-layouts, pool_pairs(): return (0.5 * (paired[..., 0, :] + paired[..., 1, :])).astype(jnp.bfloat16)  8.59 us
    select_n x14, other arithmetic, on_device(): jnp.where(active, jnp.concatenate([theirs, mine], axis=1), jnp.concatenat...  7.53 us
    dot_general x1, matrix products, on_device(): lax.dot_general(w_out, stacked, (((0,), (1,)), ((), ())), preferred_eleme...  6.51 us
    convert_element_type x26, other arithmetic, pool_pairs(): return (0.5 * (paired[..., 0, :] + paired[..., 1, :])).astype(jnp.bfloat16)  5.99 us
    dot_general x6, matrix products, level_terms(): jnp.einsum(form, queries, tan_k, preferred_element_type=jnp.float32)  5.17 us
    dot_general x6, matrix products, level_terms(): jnp.einsum(mixing, weights, tan_v, preferred_element_type=jnp.float32)  5.06 us
  transfers between devices with their start and end apart: 21, of which 2 were waited for; matrix products, arithmetic and copies ran while one was open for 32% of the time, Pallas kernels for 0%

commit v1 on v0

v1 whole, which is shorter than its diff:
```python
import math

import jax
import jax.numpy as jnp
from jax import lax
from jax.experimental import pallas as pl
from jax.experimental.pallas import tpu as pltpu
from jax.sharding import PartitionSpec as P

HD = 128
NX = 4
NZ = 8
NY = 4
HEADS_HERE = 4
LEAF = 256
MASKED = -1e30
LOG_TWO = math.log(2.0)
SCALE = 1.0 / math.sqrt(HD)
F32 = jnp.float32
BF16 = jnp.bfloat16
VMEM = pl.BlockSpec(memory_space=pltpu.VMEM)
SMEM = pl.BlockSpec(memory_space=pltpu.SMEM)
PARAMS = pltpu.CompilerParams(vmem_limit_bytes=40 * 1024 * 1024)


def dot(a, b):
    return lax.dot_general(a, b, (((1,), (0,)), ((), ())), preferred_element_type=F32)


def dot_nt(a, b):
    return lax.dot_general(a, b, (((1,), (1,)), ((), ())), preferred_element_type=F32)


def pool_matrix(rows):
    out = lax.broadcasted_iota(jnp.int32, (rows, 2 * rows), 0)
    src = lax.broadcasted_iota(jnp.int32, (rows, 2 * rows), 1)
    return jnp.where((src >> 1) == out, 0.5, 0.0).astype(BF16)


def pool(array):
    return dot(pool_matrix(array.shape[0] // 2), array).astype(BF16)


def attend(qq, kv, offset, mask=None):
    scores = dot_nt(qq[:, :HD], kv[:, HD : 2 * HD]) * SCALE + offset
    slopes = dot_nt(qq, kv[:, : 2 * HD]) * SCALE
    if mask is not None:
        scores = jnp.where(mask, scores, MASKED)
    top = jnp.max(scores, axis=1, keepdims=True)
    probs = jnp.exp(scores - top)
    moved = probs * slopes
    den = jnp.sum(probs, axis=1, keepdims=True)
    curv = jnp.sum(moved, axis=1, keepdims=True)
    both = dot(probs.astype(BF16), kv[:, 2 * HD : 4 * HD])
    acc = dot(moved.astype(BF16), kv[:, 2 * HD : 3 * HD]) + both[:, HD:]
    inv = 1.0 / den
    att = both[:, :HD] * inv
    curv = curv * inv
    tan = acc * inv - att * curv
    return att, tan, curv, top + jnp.log(den)


def merge(one, two):
    att1, tan1, curv1, lse1 = one
    att2, tan2, curv2, lse2 = two
    top = jnp.maximum(lse1, lse2)
    e1 = jnp.exp(lse1 - top)
    e2 = jnp.exp(lse2 - top)
    den = e1 + e2
    inv = 1.0 / den
    w1 = e1 * inv
    w2 = e2 * inv
    att = w1 * att1 + w2 * att2
    tan = w1 * tan1 + w2 * tan2 + (w1 * w2) * ((att1 - att2) * (curv1 - curv2))
    return att, tan, w1 * curv1 + w2 * curv2, top + jnp.log(den)


def wide(stats):
    att, tan, curv, lse = stats
    return att, tan, jnp.broadcast_to(curv, att.shape), jnp.broadcast_to(lse, att.shape)


def double(stats, scratch):
    rows = stats[0].shape[0]
    for num, part in enumerate(stats):
        scratch[num, pl.ds(0, rows, 2), :] = part
        scratch[num, pl.ds(1, rows, 2), :] = part
    return tuple(scratch[num, 0 : 2 * rows, :] for num in range(4))


def pool_kernel(place, q, tq, tk, k, v, tv, o0, o1, o2, o3):
    x = place[1]
    matrix = pool_matrix(128)
    for step, out in ((1, o1), (3, o3), (2, o2), (0, o0)):
        head = lax.rem(x + step, NX)
        cols = pl.ds(pl.multiple_of(head * HD, HD), HD)
        for num, ref in enumerate((q, tq, tk, k, v, tv)):
            out[:, num * HD : (num + 1) * HD] = dot(matrix, ref[:, cols]).astype(BF16)


def leaf_kernel(q, tq, tk, k, v, tv, att_out, tan_out, stat_out):
    row = lax.broadcasted_iota(jnp.int32, (LEAF, LEAF), 0)
    col = lax.broadcasted_iota(jnp.int32, (LEAF, LEAF), 1)
    lane = lax.broadcasted_iota(jnp.int32, (LEAF, HD), 1)
    for head in range(HEADS_HERE):
        cols = slice(head * HD, (head + 1) * HD)
        qq = jnp.concatenate([q[:, cols], tq[:, cols]], axis=1)
        kv = jnp.concatenate([tk[:, cols], k[:, cols], v[:, cols], tv[:, cols]], axis=1)
        att, tan, curv, lse = attend(qq, kv, 0.0, row >= col)
        att_out[head] = att
        tan_out[head] = tan
        stat_out[head] = jnp.where(lane == 0, lse, curv)


def upper_kernel(place, r0, r1, r2, r3, l1, l2, q3, q4, q5, k3, k4, k5):
    x = place[1]
    for step, ref in enumerate((r0, r1, r2, r3)):
        at = lax.rem(x + NX - step, NX)
        l1[pl.ds(pl.multiple_of(at * 128, 128), 128), :] = ref[...]
    level2 = pool(l1[...])
    l2[...] = level2
    level3 = pool(level2)
    q3[...] = level3[:, : 2 * HD]
    k3[...] = level3[:, 2 * HD :]
    level4 = pool(level3)
    q4[...] = level4[:, : 2 * HD]
    k4[...] = level4[:, 2 * HD :]
    level5 = pool(level4)
    q5[...] = level5[:, : 2 * HD]
    k5[...] = level5[:, 2 * HD :]


def near_kernel(l1, l2, att_out, tan_out, stat_out):
    lane = lax.broadcasted_iota(jnp.int32, (128, HD), 1)
    work = (
        (l1, 128, 0, LOG_TWO),
        (l1, 384, 256, LOG_TWO),
        (l2, 128, 0, 2 * LOG_TWO),
    )
    for num, (ref, mine, before, offset) in enumerate(work):
        att, tan, curv, lse = attend(
            ref[mine : mine + 128, : 2 * HD], ref[before : before + 128, 2 * HD :], offset
        )
        att_out[num] = att
        tan_out[num] = tan
        stat_out[num] = jnp.where(lane == 0, lse, curv)


def far_kernel(
    place, q3, q4, q5, g3, g4a, g4b, g5a, g5b, g5c, g5d, n_att, n_tan, n_stat,
    o0, o1, o2, o3, scratch, packed,
):
    x = place[1]
    z = place[0]

    def level(q, parts, number, bit):
        kv = parts[0][...] if len(parts) == 1 else jnp.concatenate([p[...] for p in parts], axis=0)
        att, tan, curv, lse = wide(attend(q[...], kv, number * LOG_TWO))
        seen = ((z >> bit) & 1) == 1
        return att, tan, curv, jnp.where(seen, lse, MASKED)

    def near(num):
        stat = n_stat[num]
        return wide((n_att[num], n_tan[num], stat[:, 1:2], stat[:, 0:1]))

    carry = level(q5, (g5a, g5b, g5c, g5d), 5, 2)
    carry = merge(level(q4, (g4a, g4b), 4, 1), double(carry, scratch))
    carry = merge(level(q3, (g3,), 3, 0), double(carry, scratch))
    first = double(carry, scratch)
    low = tuple(part[:128] for part in first)
    high = merge(near(2), tuple(part[128:] for part in first))
    lane = lax.broadcasted_iota(jnp.int32, (128, HD), 1)
    for half, stats in enumerate((low, high)):
        all_rows = double(stats, scratch)
        pieces = (
            tuple(part[:128] for part in all_rows),
            merge(near(half), tuple(part[128:] for part in all_rows)),
        )
        for num, (att, tan, curv, lse) in enumerate(pieces):
            rows = slice((2 * half + num) * 128, (2 * half + num + 1) * 128)
            packed[rows, 0:HD] = att.astype(BF16)
            packed[rows, HD : 2 * HD] = tan.astype(BF16)
            stat = jnp.zeros((128, HD), F32)
            at = 0
            for value in (lse, curv):
                for _ in range(3):
                    piece = value.astype(BF16).astype(F32)
                    stat = jnp.where(lane == at, piece, stat)
                    value = value - piece
                    at += 1
            packed[rows, 2 * HD : 3 * HD] = stat.astype(BF16)
    for step, out in enumerate((o0, o1, o2, o3)):
        to = lax.rem(x + step, NX)
        out[...] = packed[pl.ds(pl.multiple_of(to * 128, 128), 128), :]


def finish_kernel(place, b0, b1, b2, b3, l_att, l_tan, l_stat, out, scratch):
    x = place[1]
    for step, ref in enumerate((b0, b1, b2, b3)):
        head = lax.rem(x + NX - step, NX)
        stat = ref[:, 2 * HD : 3 * HD].astype(F32)
        lse = stat[:, 0:1] + stat[:, 1:2] + stat[:, 2:3]
        curv = stat[:, 3:4] + stat[:, 4:5] + stat[:, 5:6]
        rest = wide((ref[:, 0:HD].astype(F32), ref[:, HD : 2 * HD].astype(F32), curv, lse))
        rest = double(rest, scratch)
        mine = l_stat[head]
        leaf = wide((l_att[head], l_tan[head], mine[:, 1:2], mine[:, 0:1]))
        att, tan, _, _ = merge(leaf, rest)
        cols = pl.ds(pl.multiple_of(head * HD, HD), HD)
        out[0:LEAF, cols] = att.astype(BF16)
        out[LEAF : 2 * LEAF, cols] = tan.astype(BF16)


def weight_kernel(place, w_mine, w_other, mine, other):
    mine[0] = w_mine[...].T
    other[0] = w_other[...].T


def project(w1, w2, a1, a2):
    return dot_nt(w1, a1[...]) + dot_nt(w2, a2[...])


def far_chunk_kernel(w1, w2, a1, a2, half_a, half_b):
    both = project(w1[0], w2[0], a1, a2).astype(BF16)
    half_a[...] = both[:256]
    half_b[...] = both[256:]


def near_chunk_kernel(u1, u2, d1, d2, a1, a2, up_b, down_a):
    up_b[...] = project(u1[0, 256:], u2[0, 256:], a1, a2).astype(BF16)
    down_a[...] = project(d1[0, :256], d2[0, :256], a1, a2).astype(BF16)


def own_chunk_kernel(u1, u2, d1, d2, m1, m2, a1, a2, up_a, down_b, own):
    up_a[...] = project(u1[0, :256], u2[0, :256], a1, a2)
    down_b[...] = project(d1[0, 256:], d2[0, 256:], a1, a2)
    own[...] = project(m1[0], m2[0], a1, a2)


def relay_kernel(up_a, got_a, down_b, got_b, send_up, send_down):
    send_up[...] = (up_a[...] + got_a[...].astype(F32)).astype(BF16)
    send_down[...] = (down_b[...] + got_b[...].astype(F32)).astype(BF16)


def total_kernel(own, from_down_a, from_up_a, from_down_b, from_up_b, out, out_tan):
    top = own[:256] + from_down_a[...].astype(F32) + from_up_a[...].astype(F32)
    low = own[256:] + from_down_b[...].astype(F32) + from_up_b[...].astype(F32)
    out[0:256] = top[:, :256].astype(BF16)
    out[256:] = low[:, :256].astype(BF16)
    out_tan[0:256] = top[:, 256:].astype(BF16)
    out_tan[256:] = low[:, 256:].astype(BF16)


def shape(dims, kind=BF16):
    return jax.ShapeDtypeStruct(dims, kind)


def call(kernel, outs, specs, name, flops, size, scratch=(), out_specs=None, grid=()):
    return pl.pallas_call(
        kernel,
        out_shape=outs,
        in_specs=specs,
        out_specs=jax.tree.map(lambda _: VMEM, outs) if out_specs is None else out_specs,
        scratch_shapes=list(scratch),
        grid=grid,
        compiler_params=PARAMS,
        cost_estimate=pl.CostEstimate(flops=flops, bytes_accessed=size, transcendentals=0),
        name=name,
    )


def x_route(step):
    return [(z * NX + x, z * NX + (x + step) % NX) for z in range(NZ) for x in range(NX)]


def z_route(flip, bit):
    return [
        (z * NX + x, (z ^ flip) * NX + x)
        for z in range(NZ)
        if not (z >> bit) & 1
        for x in range(NX)
    ]


def y_route(step):
    return [(y * 2 + c, ((y + step) % NY) * 2 + c) for y in range(NY) for c in range(2)]


def core_route():
    return [(i, i ^ 1) for i in range(2 * NY)]


def after(first, *rest):
    return lax.optimization_barrier((first,) + rest)


def on_device(queries, keys, values, tan_queries, tan_keys, tan_values, w_out):
    ctx = lax.axis_index("ctx")
    head = lax.axis_index("head")
    place = jnp.stack([ctx // NX, ctx % NX, head // 2, head % 2]).astype(jnp.int32)
    packed_in = (queries, tan_queries, tan_keys, keys, values, tan_values)

    level1 = shape((128, 6 * HD))
    o0, o1, o2, o3 = call(
        pool_kernel, (level1,) * 4, [SMEM] + [VMEM] * 6, "pool", 10**9, 3 * 2**20
    )(place, *packed_in)
    r1 = lax.ppermute(o1, "ctx", x_route(1))
    r3 = lax.ppermute(o3, "ctx", x_route(3))
    r2 = lax.ppermute(o2, "ctx", x_route(2))

    _, *leaf_in = after(o1, *packed_in)
    leaf = call(
        leaf_kernel,
        (shape((4, LEAF, HD), F32),) * 3,
        [VMEM] * 6,
        "leaf",
        3 * 10**9,
        4 * 2**20,
    )(*leaf_in)
    _, w_later = after(o1, w_out)
    w_mine, w_other = pl.pallas_call(
        weight_kernel,
        out_shape=(shape((NY, 512, 512)),) * 2,
        grid_spec=pltpu.PrefetchScalarGridSpec(
            num_scalar_prefetch=1,
            grid=(NY,),
            in_specs=[
                pl.BlockSpec((512, 512), lambda j, p: (0, ((p[2] + j) % NY) * 2 + p[3])),
                pl.BlockSpec((512, 512), lambda j, p: (0, ((p[2] + j) % NY) * 2 + 1 - p[3])),
            ],
            out_specs=[pl.BlockSpec((1, 512, 512), lambda j, p: (j, 0, 0))] * 2,
        ),
        compiler_params=PARAMS,
        cost_estimate=pl.CostEstimate(flops=0, bytes_accessed=10 * 2**20, transcendentals=0),
        name="weights",
    )(place, w_later, w_later)
    w_pair = lax.ppermute(w_other, "head", core_route())

    l1, l2, q3, q4, q5, k3, k4, k5 = call(
        upper_kernel,
        (
            shape((512, 6 * HD)),
            shape((256, 6 * HD)),
            shape((128, 2 * HD)),
            shape((64, 2 * HD)),
            shape((32, 2 * HD)),
            shape((128, 4 * HD)),
            shape((64, 4 * HD)),
            shape((32, 4 * HD)),
        ),
        [SMEM] + [VMEM] * 4,
        "upper",
        10**9,
        3 * 2**20,
    )(place, o0, r1, r2, r3)
    g4 = [lax.ppermute(k4, "ctx", z_route(flip, 1)) for flip in (2, 3)]
    g5 = [lax.ppermute(k5, "ctx", z_route(flip, 2)) for flip in (4, 5, 6, 7)]
    g3 = lax.ppermute(k3, "ctx", z_route(1, 0))
    near = call(
        near_kernel,
        (shape((3, 128, HD), F32),) * 3,
        [VMEM] * 2,
        "near",
        10**9,
        2 * 2**20,
    )(l1, l2)
    back = shape((128, 3 * HD))
    s0, s1, s2, s3 = call(
        far_kernel,
        (back,) * 4,
        [SMEM] + [VMEM] * 13,
        "far",
        10**9,
        2 * 2**20,
        scratch=[pltpu.VMEM((4, 256, HD), F32), pltpu.VMEM((512, 3 * HD), BF16)],
    )(place, q3, q4, q5, g3, *g4, *g5, *near)
    b1 = lax.ppermute(s1, "ctx", x_route(1))
    b3 = lax.ppermute(s3, "ctx", x_route(3))
    b2 = lax.ppermute(s2, "ctx", x_route(2))

    rows = 2 * LEAF
    mine = call(
        finish_kernel,
        shape((rows, 4 * HD)),
        [SMEM] + [VMEM] * 7,
        "finish",
        10**8,
        3 * 2**20,
        scratch=[pltpu.VMEM((4, 256, HD), F32)],
    )(place, s0, b1, b2, b3, *leaf)
    pair = lax.ppermute(mine, "head", core_route())

    def chunk(j):
        return pl.BlockSpec((1, 512, 512), lambda i, j=j: (j, 0, 0))

    whole = pl.BlockSpec((rows, 4 * HD), lambda i: (0, 0))
    half = pl.BlockSpec((256, rows), lambda i: (0, 0))
    full = pl.BlockSpec((512, rows), lambda i: (0, 0))
    far_a, far_b = call(
        far_chunk_kernel,
        (shape((256, rows)),) * 2,
        [chunk(2)] * 2 + [whole] * 2,
        "chunk_far",
        5 * 10**8,
        2 * 2**20,
        out_specs=(half,) * 2,
        grid=(1,),
    )(w_mine, w_pair, mine, pair)
    got_a = lax.ppermute(far_a, "head", y_route(1))
    got_b = lax.ppermute(far_b, "head", y_route(3))
    _, mine2, pair2 = after(far_a, mine, pair)
    up_b, down_a = call(
        near_chunk_kernel,
        (shape((256, rows)),) * 2,
        [chunk(1)] * 2 + [chunk(3)] * 2 + [whole] * 2,
        "chunk_near",
        5 * 10**8,
        3 * 2**20,
        out_specs=(half,) * 2,
        grid=(1,),
    )(w_mine, w_pair, w_mine, w_pair, mine2, pair2)
    from_down_b = lax.ppermute(up_b, "head", y_route(1))
    from_up_a = lax.ppermute(down_a, "head", y_route(3))
    _, mine3, pair3 = after(up_b, mine, pair)
    up_a, down_b, own = call(
        own_chunk_kernel,
        (shape((256, rows), F32),) * 2 + (shape((512, rows), F32),),
        [chunk(1)] * 2 + [chunk(3)] * 2 + [chunk(0)] * 2 + [whole] * 2,
        "chunk_own",
        10**9,
        5 * 2**20,
        out_specs=(half, half, full),
        grid=(1,),
    )(w_mine, w_pair, w_mine, w_pair, w_mine, w_pair, mine3, pair3)
    send_up, send_down = call(
        relay_kernel, (shape((256, rows)),) * 2, [VMEM] * 4, "relay", 10**6, 2 * 2**20
    )(up_a, got_a, down_b, got_b)
    from_down_a = lax.ppermute(send_up, "head", y_route(1))
    from_up_b = lax.ppermute(send_down, "head", y_route(3))
    return call(
        total_kernel,
        (shape((512, LEAF)),) * 2,
        [VMEM] * 5,
        "total",
        10**6,
        3 * 2**20,
    )(own, from_down_a, from_up_a, from_down_b, from_up_b)


def solution(mesh):
    return jax.shard_map(
        on_device,
        mesh=mesh,
        in_specs=(P("ctx", "head"),) * 6 + (P("head", None),),
        out_specs=(P("head", "ctx"), P("head", "ctx")),
        check_vma=False,
    )
```

time: 191 us -> 94.9 us (0.50); the launches traced: 188 us -> 94.5 us
  matrix products: 25.5 us -> 0 us
  other arithmetic: 25.5 us -> 0.08 us
  local copies, waits for them, and re-layouts: 24 us -> 7.92 us
  waiting for transfers between devices: 40.1 us -> 24.8 us
  Pallas kernels: 0 us -> 14.6 us
  between operations: 15 us -> 0.94 us
  starting transfers between devices: 57.9 us -> 46.1 us
    reduce_scatter x1 -> x0, waiting for transfers between devices: 39 us -> none  [on_device(): lax.psum_scatter(lax.dot_general(w_out, stacked, (((0,), (1,)), ((), ()))...]
    dot_general x37 -> x0, matrix products: 25.5 us -> none  [the longest x1 6.51 us: on_device(): lax.dot_general(w_out, stacked, (((0,), (1,)), ((), ())), preferred_eleme...]
    ppermute x20 -> x21, waiting for transfers between devices: 1.04 us -> 24.8 us  [the longest x1 5.62 us: on_device(): from_down_a = lax.ppermute(send_up, 'head', y_route(1))]
    pallas_call x0 -> x12, Pallas kernels: none -> 14.6 us  [the longest x1 2.31 us: on_device(): pl.pallas_call(weight_kernel, out_shape=(shape((NY, 512, 512)),) * 2, gri...]
    convert_element_type x33 -> x0, other arithmetic: 11.9 us -> none  [the longest x26 5.99 us: pool_pairs(): return (0.5 * (paired[..., 0, :] + paired[..., 1, :])).astype(jnp.bfloat16)]
    ppermute x20 -> x21, starting transfers between devices: 57.9 us -> 46.1 us  [the longest x4 14.1 us: on_device(): g5 = [lax.ppermute(k5, 'ctx', z_route(flip, 2)) for flip in (4, 5, 6, 7)]]
    slice x29 -> x0, local copies, waits for them, and re-layouts: 9.73 us -> none  [the longest x24 8.59 us: pool_pairs(): return (0.5 * (paired[..., 0, :] + paired[..., 1, :])).astype(jnp.bfloat16)]
    select_n x19 -> x0, other arithmetic: 7.56 us -> none  [the longest x14 7.53 us: on_device(): jnp.where(active, jnp.concatenate([theirs, mine], axis=1), jnp.concatenat...]
  transfers between devices with their start and end apart: 21 -> 21, of which waited for: 2 -> 11; matrix products, arithmetic and copies ran while one was open for 32% -> 0% of each run, Pallas kernels for 0% -> 10%
where the time goes in v1:
time: 94.9 us; the launch traced here: 94.5 us
  starting transfers between devices  46.1 us (49%)
  waiting for transfers between devices  24.8 us (26%)
  Pallas kernels  14.6 us (15%)
  local copies, waits for them, and re-layouts  7.92 us (8%)
    ppermute x4, starting transfers between devices, on_device(): g5 = [lax.ppermute(k5, 'ctx', z_route(flip, 2)) for flip in (4, 5, 6, 7)]  14.1 us
    unnamed x26, local copies, waits for them, and re-layouts  7.92 us
    ppermute x2, starting transfers between devices, on_device(): g4 = [lax.ppermute(k4, 'ctx', z_route(flip, 1)) for flip in (2, 3)]  5.84 us
    ppermute x1, waiting for transfers between devices, on_device(): from_down_a = lax.ppermute(send_up, 'head', y_route(1))  5.62 us
    ppermute x1, waiting for transfers between devices, on_device(): r2 = lax.ppermute(o2, 'ctx', x_route(2))  5.52 us
    ppermute x1, starting transfers between devices, on_device(): pair = lax.ppermute(mine, 'head', core_route())  5.11 us
    ppermute x1, starting transfers between devices, on_device(): w_pair = lax.ppermute(w_other, 'head', core_route())  3.33 us
    ppermute x1, waiting for transfers between devices, on_device(): got_a = lax.ppermute(far_a, 'head', y_route(1))  3.09 us
  transfers between devices with their start and end apart: 21, of which 11 were waited for; matrix products, arithmetic and copies ran while one was open for 0% of the time, Pallas kernels for 10%

profile of v1, /device:TPU:1, one launch (start us, length us, event | category | flops | bytes accessed | tf_op | source)
XLA Modules:
  0.0 94.5 jit_solution(11307059069687278374)
XLA Ops:
  7.6 2.2 %copy-done = bf16[512,4096]{1,0:T(8,128)(2,1)S(1)} copy-done((bf16[512,4096]{1,0:T(8,128)(2,1)S(1)}, bf16[512,4096]{1,0:T(8,128)(2,1)}, u32[]{:S(2)}) %copy-start) | copy-done | bytes 4194328
  9.8 2.3 %weights.1 = (bf16[4,512,512]{2,1,0:T(8,128)(2,1)S(1)}, bf16[4,512,512]{2,1,0:T(8,128)(2,1)S(1)}) custom-call(s32[4]{0:T(128)S(1)} %pad_add_fusion.place, bf16[512,4096]{1,0:T(8,128)(2,1)S(1)} %copy-done, bf16[512,4096]{1,0:T(8,128)(2,1)S(1)} %copy-done), custom_call_target="tpu_custom_call" | custom-call | bytes 10485760 | tf_op jit(solution)/shard_map/weights/pallas_call | solution.py:321
  12.1 3.3 %collective-permute-start = (bf16[4,512,512]{2,1,0:T(8,128)(2,1)S(1)}, bf16[4,512,512]{2,1,0:T(8,128)(2,1)S(1)}, u32[]{:S(2)}, u32[]{:S(2)}) collective-permute-start(bf16[4,512,512]{2,1,0:T(8,128)(2,1)S(1)} %get-tuple-element.49), channel_id=1, source_target_pairs={{0,1},{1,0},{2,3},{3,2},{4,5},{5,4},{6,7},{7,6},{8,9},{9,8},{10,11... | collective-permute-start | bytes 6291464 | tf_op jit(solution)/shard_map/ppermute | solution.py:337
  17.9 5.5 %collective-permute-done.2.r2 = bf16[128,768]{1,0:T(8,128)(2,1)S(1)} collective-permute-done((bf16[128,768]{1,0:T(8,128)(2,1)S(1)}, bf16[128,768]{1,0:T(8,128)(2,1)S(1)}, u32[]{:S(2)}, u32[]{:S(2)}) %collective-permute-start.2) | collective-permute-done | bytes 196640 | tf_op jit(solution)/shard_map/ppermute | solution.py:309
  23.4 2.6 %collective-permute-done.3.r3 = bf16[128,768]{1,0:T(8,128)(2,1)S(1)} collective-permute-done((bf16[128,768]{1,0:T(8,128)(2,1)S(1)}, bf16[128,768]{1,0:T(8,128)(2,1)S(1)}, u32[]{:S(2)}, u32[]{:S(2)}) %collective-permute-start.3) | collective-permute-done | bytes 196640 | tf_op jit(solution)/shard_map/ppermute | solution.py:308
  26.0 2.0 %collective-permute-done.1.r1 = bf16[128,768]{1,0:T(8,128)(2,1)S(1)} collective-permute-done((bf16[128,768]{1,0:T(8,128)(2,1)S(1)}, bf16[128,768]{1,0:T(8,128)(2,1)S(1)}, u32[]{:S(2)}, u32[]{:S(2)}) %collective-permute-start.1) | collective-permute-done | bytes 196640 | tf_op jit(solution)/shard_map/ppermute | solution.py:307
  29.4 1.6 %collective-permute-start.4 = (bf16[128,512]{1,0:T(8,128)(2,1)S(1)}, bf16[128,512]{1,0:T(8,128)(2,1)S(1)}, u32[]{:S(2)}, u32[]{:S(2)}) collective-permute-start(bf16[128,512]{1,0:T(8,128)(2,1)S(1)} %get-tuple-element.56), channel_id=1, source_target_pairs={{0,32},{8,40},{16,48},{24,56},{64,96},{72,104},{80,112},{88,120},{... | collective-permute-start | bytes 393224 | tf_op jit(solution)/shard_map/ppermute | solution.py:358
  31.0 5.2 %collective-permute-start.10 = (bf16[32,512]{1,0:T(8,128)(2,1)S(1)}, bf16[32,512]{1,0:T(8,128)(2,1)S(1)}, u32[]{:S(2)}, u32[]{:S(2)}) collective-permute-start(bf16[32,512]{1,0:T(8,128)(2,1)S(1)} %get-tuple-element.58), channel_id=1, source_target_pairs={{0,224},{8,232},{16,240},{24,248},{32,192},{40,200},{48,208},{56,2... | collective-permute-start | bytes 98312 | tf_op jit(solution)/shard_map/ppermute | solution.py:357
  36.2 3.1 %collective-permute-start.9 = (bf16[32,512]{1,0:T(8,128)(2,1)S(1)}, bf16[32,512]{1,0:T(8,128)(2,1)S(1)}, u32[]{:S(2)}, u32[]{:S(2)}) collective-permute-start(bf16[32,512]{1,0:T(8,128)(2,1)S(1)} %get-tuple-element.58), channel_id=1, source_target_pairs={{0,192},{8,200},{16,208},{24,216},{32,224},{40,232},{48,240},{56,2... | collective-permute-start | bytes 98312 | tf_op jit(solution)/shard_map/ppermute | solution.py:357
  40.6 4.5 %collective-permute-start.7 = (bf16[32,512]{1,0:T(8,128)(2,1)S(1)}, bf16[32,512]{1,0:T(8,128)(2,1)S(1)}, u32[]{:S(2)}, u32[]{:S(2)}) collective-permute-start(bf16[32,512]{1,0:T(8,128)(2,1)S(1)} %get-tuple-element.58), channel_id=1, source_target_pairs={{0,128},{8,136},{16,144},{24,152},{32,160},{40,168},{48,176},{56,1... | collective-permute-start | bytes 98312 | tf_op jit(solution)/shard_map/ppermute | solution.py:357
  45.1 1.8 %collective-permute-start.6 = (bf16[64,512]{1,0:T(8,128)(2,1)S(1)}, bf16[64,512]{1,0:T(8,128)(2,1)S(1)}, u32[]{:S(2)}, u32[]{:S(2)}) collective-permute-start(bf16[64,512]{1,0:T(8,128)(2,1)S(1)} %get-tuple-element.57), channel_id=1, source_target_pairs={{0,96},{8,104},{16,112},{24,120},{32,64},{40,72},{48,80},{56,88},{... | collective-permute-start | bytes 196616 | tf_op jit(solution)/shard_map/ppermute | solution.py:356
  47.0 4.0 %collective-permute-start.5 = (bf16[64,512]{1,0:T(8,128)(2,1)S(1)}, bf16[64,512]{1,0:T(8,128)(2,1)S(1)}, u32[]{:S(2)}, u32[]{:S(2)}) collective-permute-start(bf16[64,512]{1,0:T(8,128)(2,1)S(1)} %get-tuple-element.57), channel_id=1, source_target_pairs={{0,64},{8,72},{16,80},{24,88},{32,96},{40,104},{48,112},{56,120},{... | collective-permute-start | bytes 196616 | tf_op jit(solution)/shard_map/ppermute | solution.py:356
  52.3 2.0 %far.1 = (bf16[128,384]{1,0:T(8,128)(2,1)S(1)}, bf16[128,384]{1,0:T(8,128)(2,1)S(1)}, bf16[128,384]{1,0:T(8,128)(2,1)S(1)}, bf16[128,384]{1,0:T(8,128)(2,1)S(1)}) custom-call(s32[4]{0:T(128)S(1)} %pad_add_fusion.place, bf16[128,256]{1,0:T(8,128)(2,1)S(1)} %get-tuple-element.53.q3, bf16[64,256]{1,0:T(8,128)(2,1)S(1)} %get-tuple-element.54.q4, ...), custom_call_target="tpu_custom_call" | custom-call | flops 1000000000 | bytes 2097152 | tf_op jit(solution)/shard_map/far/pallas_call | solution.py:368
  54.4 1.6 %collective-permute-start.11 = (bf16[128,384]{1,0:T(8,128)(2,1)S(1)}, bf16[128,384]{1,0:T(8,128)(2,1)S(1)}, u32[]{:S(2)}, u32[]{:S(2)}) collective-permute-start(bf16[128,384]{1,0:T(8,128)(2,1)S(1)} %get-tuple-element.65), channel_id=1, source_target_pairs={{0,8},{8,16},{16,24},{24,0},{32,40},{40,48},{48,56},{56,32},{64,72... | collective-permute-start | bytes 294920 | tf_op jit(solution)/shard_map/ppermute | solution.py:377
  55.9 2.5 %collective-permute-start.12 = (bf16[128,384]{1,0:T(8,128)(2,1)S(1)}, bf16[128,384]{1,0:T(8,128)(2,1)S(1)}, u32[]{:S(2)}, u32[]{:S(2)}) collective-permute-start(bf16[128,384]{1,0:T(8,128)(2,1)S(1)} %get-tuple-element.66), channel_id=1, source_target_pairs={{0,16},{8,24},{16,0},{24,8},{32,48},{40,56},{48,32},{56,40},{64,80... | collective-permute-start | bytes 294920 | tf_op jit(solution)/shard_map/ppermute | solution.py:379
  61.8 1.7 %finish.1.a1 = bf16[512,512]{1,0:T(8,128)(2,1)S(1)} custom-call(s32[4]{0:T(128)S(1)} %pad_add_fusion.place, bf16[128,384]{1,0:T(8,128)(2,1)S(1)} %get-tuple-element.64.b0, bf16[128,384]{1,0:T(8,128)(2,1)S(1)} %collective-permute-done.11.b1, bf16[128,384]{1,0:T(8,128)(2,1)S(1)} %collective-permute-done.12.b2, ...), custom_call_target="tpu_custom_call" | custom-call | flops 100000000 | bytes 3145728 | tf_op jit(solution)/shard_map/finish/pallas_call | solution.py:382
  63.6 5.1 %collective-permute-start.14 = (bf16[512,512]{1,0:T(8,128)(2,1)S(1)}, bf16[512,512]{1,0:T(8,128)(2,1)S(1)}, u32[]{:S(2)}, u32[]{:S(2)}) collective-permute-start(bf16[512,512]{1,0:T(8,128)(2,1)S(1)} %finish.1.a1), channel_id=1, source_target_pairs={{0,1},{1,0},{2,3},{3,2},{4,5},{5,4},{6,7},{7,6},{8,9},{9,8},{10,11... | collective-permute-start | bytes 1572872 | tf_op jit(solution)/shard_map/ppermute | solution.py:391
  68.7 1.5 %collective-permute-done.14.a2 = bf16[512,512]{1,0:T(8,128)(2,1)S(1)} collective-permute-done((bf16[512,512]{1,0:T(8,128)(2,1)S(1)}, bf16[512,512]{1,0:T(8,128)(2,1)S(1)}, u32[]{:S(2)}, u32[]{:S(2)}) %collective-permute-start.14) | collective-permute-done | bytes 524320 | tf_op jit(solution)/shard_map/ppermute | solution.py:391
  71.0 3.0 %collective-permute-start.16 = (bf16[256,512]{1,0:T(8,128)(2,1)S(1)}, bf16[256,512]{1,0:T(8,128)(2,1)S(1)}, u32[]{:S(2)}, u32[]{:S(2)}) collective-permute-start(bf16[256,512]{1,0:T(8,128)(2,1)S(1)} %get-tuple-element.86), channel_id=1, source_target_pairs={{0,6},{1,7},{2,0},{3,1},{4,2},{5,3},{6,4},{7,5},{8,14},{9,15},{10,... | collective-permute-start | bytes 786440 | tf_op jit(solution)/shard_map/ppermute | solution.py:410
  74.8 2.7 %collective-permute-start.18 = (bf16[256,512]{1,0:T(8,128)(2,1)S(1)}, bf16[256,512]{1,0:T(8,128)(2,1)S(1)}, u32[]{:S(2)}, u32[]{:S(2)}) collective-permute-start(bf16[256,512]{1,0:T(8,128)(2,1)S(1)} %get-tuple-element.88), channel_id=1, source_target_pairs={{0,6},{1,7},{2,0},{3,1},{4,2},{5,3},{6,4},{7,5},{8,14},{9,15},{10,... | collective-permute-start | bytes 786440 | tf_op jit(solution)/shard_map/ppermute | solution.py:423
  79.3 3.1 %collective-permute-done.15.got_a = bf16[256,512]{1,0:T(8,128)(2,1)S(1)} collective-permute-done((bf16[256,512]{1,0:T(8,128)(2,1)S(1)}, bf16[256,512]{1,0:T(8,128)(2,1)S(1)}, u32[]{:S(2)}, u32[]{:S(2)}) %collective-permute-start.15) | collective-permute-done | bytes 262176 | tf_op jit(solution)/shard_map/ppermute | solution.py:409
  82.6 2.7 %collective-permute-start.20 = (bf16[256,512]{1,0:T(8,128)(2,1)S(1)}, bf16[256,512]{1,0:T(8,128)(2,1)S(1)}, u32[]{:S(2)}, u32[]{:S(2)}) collective-permute-start(bf16[256,512]{1,0:T(8,128)(2,1)S(1)} %get-tuple-element.89), channel_id=1, source_target_pairs={{0,6},{1,7},{2,0},{3,1},{4,2},{5,3},{6,4},{7,5},{8,14},{9,15},{10,... | collective-permute-start | bytes 786440 | tf_op jit(solution)/shard_map/ppermute | solution.py:439
  85.2 2.8 %collective-permute-done.19.from_down_b = bf16[256,512]{1,0:T(8,128)(2,1)S(1)} collective-permute-done((bf16[256,512]{1,0:T(8,128)(2,1)S(1)}, bf16[256,512]{1,0:T(8,128)(2,1)S(1)}, u32[]{:S(2)}, u32[]{:S(2)}) %collective-permute-start.19) | collective-permute-done | bytes 262176 | tf_op jit(solution)/shard_map/ppermute | solution.py:422
  88.0 5.6 %collective-permute-done.17.from_down_a = bf16[256,512]{1,0:T(8,128)(2,1)S(1)} collective-permute-done((bf16[256,512]{1,0:T(8,128)(2,1)S(1)}, bf16[256,512]{1,0:T(8,128)(2,1)S(1)}, u32[]{:S(2)}, u32[]{:S(2)}) %collective-permute-start.17) | collective-permute-done | bytes 262176 | tf_op jit(solution)/shard_map/ppermute | solution.py:438
  (57 shorter events, 21.2 us)
Async XLA Ops:
  12.1 58.2 %collective-permute-start = (bf16[4,512,512]{2,1,0:T(8,128)(2,1)S(1)}, bf16[4,512,512]{2,1,0:T(8,128)(2,1)S(1)}, u32[]{:S(2)}, u32[]{:S(2)}) collective-permute-start(bf16[4,512,512]{2,1,0:T(8,128)(2,1)S(1)} %get-tuple-element.49), channel_id=1, source_target_pairs={{0,1},{1,0},{2,3},{3,2},{4,5},{5,4},{6,7},{7,6},{8,9},{9,8},{10,11... | collective-permute-start | bytes 6291464 | tf_op jit(solution)/shard_map/ppermute | solution.py:337
  15.4 8.0 %collective-permute-start.2 = (bf16[128,768]{1,0:T(8,128)(2,1)S(1)}, bf16[128,768]{1,0:T(8,128)(2,1)S(1)}, u32[]{:S(2)}, u32[]{:S(2)}) collective-permute-start(bf16[128,768]{1,0:T(8,128)(2,1)S(1)} %get-tuple-element.51), channel_id=1, source_target_pairs={{0,16},{8,24},{16,0},{24,8},{32,48},{40,56},{48,32},{56,40},{64,80... | collective-permute-start | bytes 589832 | tf_op jit(solution)/shard_map/ppermute | solution.py:309
  16.4 9.5 %collective-permute-start.3 = (bf16[128,768]{1,0:T(8,128)(2,1)S(1)}, bf16[128,768]{1,0:T(8,128)(2,1)S(1)}, u32[]{:S(2)}, u32[]{:S(2)}) collective-permute-start(bf16[128,768]{1,0:T(8,128)(2,1)S(1)} %get-tuple-element.52), channel_id=1, source_target_pairs={{0,24},{8,0},{16,8},{24,16},{32,56},{40,32},{48,40},{56,48},{64,88... | collective-permute-start | bytes 589832 | tf_op jit(solution)/shard_map/ppermute | solution.py:308
  17.3 10.7 %collective-permute-start.1 = (bf16[128,768]{1,0:T(8,128)(2,1)S(1)}, bf16[128,768]{1,0:T(8,128)(2,1)S(1)}, u32[]{:S(2)}, u32[]{:S(2)}) collective-permute-start(bf16[128,768]{1,0:T(8,128)(2,1)S(1)} %get-tuple-element.46), channel_id=1, source_target_pairs={{0,8},{8,16},{16,24},{24,0},{32,40},{40,48},{48,56},{56,32},{64,72... | collective-permute-start | bytes 589832 | tf_op jit(solution)/shard_map/ppermute | solution.py:307
  29.4 22.9 %collective-permute-start.4 = (bf16[128,512]{1,0:T(8,128)(2,1)S(1)}, bf16[128,512]{1,0:T(8,128)(2,1)S(1)}, u32[]{:S(2)}, u32[]{:S(2)}) collective-permute-start(bf16[128,512]{1,0:T(8,128)(2,1)S(1)} %get-tuple-element.56), channel_id=1, source_target_pairs={{0,32},{8,40},{16,48},{24,56},{64,96},{72,104},{80,112},{88,120},{... | collective-permute-start | bytes 393224 | tf_op jit(solution)/shard_map/ppermute | solution.py:358
  31.0 9.6 %collective-permute-start.10 = (bf16[32,512]{1,0:T(8,128)(2,1)S(1)}, bf16[32,512]{1,0:T(8,128)(2,1)S(1)}, u32[]{:S(2)}, u32[]{:S(2)}) collective-permute-start(bf16[32,512]{1,0:T(8,128)(2,1)S(1)} %get-tuple-element.58), channel_id=1, source_target_pairs={{0,224},{8,232},{16,240},{24,248},{32,192},{40,200},{48,208},{56,2... | collective-permute-start | bytes 98312 | tf_op jit(solution)/shard_map/ppermute | solution.py:357
  36.2 8.9 %collective-permute-start.9 = (bf16[32,512]{1,0:T(8,128)(2,1)S(1)}, bf16[32,512]{1,0:T(8,128)(2,1)S(1)}, u32[]{:S(2)}, u32[]{:S(2)}) collective-permute-start(bf16[32,512]{1,0:T(8,128)(2,1)S(1)} %get-tuple-element.58), channel_id=1, source_target_pairs={{0,192},{8,200},{16,208},{24,216},{32,224},{40,232},{48,240},{56,2... | collective-permute-start | bytes 98312 | tf_op jit(solution)/shard_map/ppermute | solution.py:357
  39.3 7.7 %collective-permute-start.8 = (bf16[32,512]{1,0:T(8,128)(2,1)S(1)}, bf16[32,512]{1,0:T(8,128)(2,1)S(1)}, u32[]{:S(2)}, u32[]{:S(2)}) collective-permute-start(bf16[32,512]{1,0:T(8,128)(2,1)S(1)} %get-tuple-element.58), channel_id=1, source_target_pairs={{0,160},{8,168},{16,176},{24,184},{32,128},{40,136},{48,144},{56,1... | collective-permute-start | bytes 98312 | tf_op jit(solution)/shard_map/ppermute | solution.py:357
  40.6 11.3 %collective-permute-start.7 = (bf16[32,512]{1,0:T(8,128)(2,1)S(1)}, bf16[32,512]{1,0:T(8,128)(2,1)S(1)}, u32[]{:S(2)}, u32[]{:S(2)}) collective-permute-start(bf16[32,512]{1,0:T(8,128)(2,1)S(1)} %get-tuple-element.58), channel_id=1, source_target_pairs={{0,128},{8,136},{16,144},{24,152},{32,160},{40,168},{48,176},{56,1... | collective-permute-start | bytes 98312 | tf_op jit(solution)/shard_map/ppermute | solution.py:357
  45.1 6.8 %collective-permute-start.6 = (bf16[64,512]{1,0:T(8,128)(2,1)S(1)}, bf16[64,512]{1,0:T(8,128)(2,1)S(1)}, u32[]{:S(2)}, u32[]{:S(2)}) collective-permute-start(bf16[64,512]{1,0:T(8,128)(2,1)S(1)} %get-tuple-element.57), channel_id=1, source_target_pairs={{0,96},{8,104},{16,112},{24,120},{32,64},{40,72},{48,80},{56,88},{... | collective-permute-start | bytes 196616 | tf_op jit(solution)/shard_map/ppermute | solution.py:356
  47.0 5.3 %collective-permute-start.5 = (bf16[64,512]{1,0:T(8,128)(2,1)S(1)}, bf16[64,512]{1,0:T(8,128)(2,1)S(1)}, u32[]{:S(2)}, u32[]{:S(2)}) collective-permute-start(bf16[64,512]{1,0:T(8,128)(2,1)S(1)} %get-tuple-element.57), channel_id=1, source_target_pairs={{0,64},{8,72},{16,80},{24,88},{32,96},{40,104},{48,112},{56,120},{... | collective-permute-start | bytes 196616 | tf_op jit(solution)/shard_map/ppermute | solution.py:356
  51.9 7.6 %copy-start.2 = (bf16[256,512]{1,0:T(8,128)(2,1)S(1)}, bf16[256,512]{1,0:T(8,128)(2,1)}, u32[]{:S(2)}) copy-start(bf16[256,512]{1,0:T(8,128)(2,1)} %q.2) | copy-start | bytes 786436
  51.9 7.6 %copy-start.4 = (bf16[256,512]{1,0:T(8,128)(2,1)S(1)}, bf16[256,512]{1,0:T(8,128)(2,1)}, u32[]{:S(2)}) copy-start(bf16[256,512]{1,0:T(8,128)(2,1)} %tq.2) | copy-start | bytes 786436
  51.9 7.6 %copy-start.6 = (bf16[256,512]{1,0:T(8,128)(2,1)S(1)}, bf16[256,512]{1,0:T(8,128)(2,1)}, u32[]{:S(2)}) copy-start(bf16[256,512]{1,0:T(8,128)(2,1)} %tk.2) | copy-start | bytes 786436
  54.4 6.6 %collective-permute-start.11 = (bf16[128,384]{1,0:T(8,128)(2,1)S(1)}, bf16[128,384]{1,0:T(8,128)(2,1)S(1)}, u32[]{:S(2)}, u32[]{:S(2)}) collective-permute-start(bf16[128,384]{1,0:T(8,128)(2,1)S(1)} %get-tuple-element.65), channel_id=1, source_target_pairs={{0,8},{8,16},{16,24},{24,0},{32,40},{40,48},{48,56},{56,32},{64,72... | collective-permute-start | bytes 294920 | tf_op jit(solution)/shard_map/ppermute | solution.py:377
  55.9 5.5 %collective-permute-start.12 = (bf16[128,384]{1,0:T(8,128)(2,1)S(1)}, bf16[128,384]{1,0:T(8,128)(2,1)S(1)}, u32[]{:S(2)}, u32[]{:S(2)}) collective-permute-start(bf16[128,384]{1,0:T(8,128)(2,1)S(1)} %get-tuple-element.66), channel_id=1, source_target_pairs={{0,16},{8,24},{16,0},{24,8},{32,48},{40,56},{48,32},{56,40},{64,80... | collective-permute-start | bytes 294920 | tf_op jit(solution)/shard_map/ppermute | solution.py:379
  58.4 3.5 %collective-permute-start.13 = (bf16[128,384]{1,0:T(8,128)(2,1)S(1)}, bf16[128,384]{1,0:T(8,128)(2,1)S(1)}, u32[]{:S(2)}, u32[]{:S(2)}) collective-permute-start(bf16[128,384]{1,0:T(8,128)(2,1)S(1)} %get-tuple-element.67), channel_id=1, source_target_pairs={{0,24},{8,0},{16,8},{24,16},{32,56},{40,32},{48,40},{56,48},{64,88... | collective-permute-start | bytes 294920 | tf_op jit(solution)/shard_map/ppermute | solution.py:378
  63.6 6.6 %collective-permute-start.14 = (bf16[512,512]{1,0:T(8,128)(2,1)S(1)}, bf16[512,512]{1,0:T(8,128)(2,1)S(1)}, u32[]{:S(2)}, u32[]{:S(2)}) collective-permute-start(bf16[512,512]{1,0:T(8,128)(2,1)S(1)} %finish.1.a1), channel_id=1, source_target_pairs={{0,1},{1,0},{2,3},{3,2},{4,5},{5,4},{6,7},{7,6},{8,9},{9,8},{10,11... | collective-permute-start | bytes 1572872 | tf_op jit(solution)/shard_map/ppermute | solution.py:391
  71.0 8.3 %collective-permute-start.16 = (bf16[256,512]{1,0:T(8,128)(2,1)S(1)}, bf16[256,512]{1,0:T(8,128)(2,1)S(1)}, u32[]{:S(2)}, u32[]{:S(2)}) collective-permute-start(bf16[256,512]{1,0:T(8,128)(2,1)S(1)} %get-tuple-element.86), channel_id=1, source_target_pairs={{0,6},{1,7},{2,0},{3,1},{4,2},{5,3},{6,4},{7,5},{8,14},{9,15},{10,... | collective-permute-start | bytes 786440 | tf_op jit(solution)/shard_map/ppermute | solution.py:410
  74.0 8.4 %collective-permute-start.15 = (bf16[256,512]{1,0:T(8,128)(2,1)S(1)}, bf16[256,512]{1,0:T(8,128)(2,1)S(1)}, u32[]{:S(2)}, u32[]{:S(2)}) collective-permute-start(bf16[256,512]{1,0:T(8,128)(2,1)S(1)} %get-tuple-element.77), channel_id=1, source_target_pairs={{0,2},{1,3},{2,4},{3,5},{4,6},{5,7},{6,0},{7,1},{8,10},{9,11},{10,... | collective-permute-start | bytes 786440 | tf_op jit(solution)/shard_map/ppermute | solution.py:409
  74.7 13.3 %collective-permute-start.19 = (bf16[256,512]{1,0:T(8,128)(2,1)S(1)}, bf16[256,512]{1,0:T(8,128)(2,1)S(1)}, u32[]{:S(2)}, u32[]{:S(2)}) collective-permute-start(bf16[256,512]{1,0:T(8,128)(2,1)S(1)} %get-tuple-element.80), channel_id=1, source_target_pairs={{0,2},{1,3},{2,4},{3,5},{4,6},{5,7},{6,0},{7,1},{8,10},{9,11},{10,... | collective-permute-start | bytes 786440 | tf_op jit(solution)/shard_map/ppermute | solution.py:422
  74.8 10.4 %collective-permute-start.18 = (bf16[256,512]{1,0:T(8,128)(2,1)S(1)}, bf16[256,512]{1,0:T(8,128)(2,1)S(1)}, u32[]{:S(2)}, u32[]{:S(2)}) collective-permute-start(bf16[256,512]{1,0:T(8,128)(2,1)S(1)} %get-tuple-element.88), channel_id=1, source_target_pairs={{0,6},{1,7},{2,0},{3,1},{4,2},{5,3},{6,4},{7,5},{8,14},{9,15},{10,... | collective-permute-start | bytes 786440 | tf_op jit(solution)/shard_map/ppermute | solution.py:423
  82.5 11.1 %collective-permute-start.17 = (bf16[256,512]{1,0:T(8,128)(2,1)S(1)}, bf16[256,512]{1,0:T(8,128)(2,1)S(1)}, u32[]{:S(2)}, u32[]{:S(2)}) collective-permute-start(bf16[256,512]{1,0:T(8,128)(2,1)S(1)} %get-tuple-element.87), channel_id=1, source_target_pairs={{0,2},{1,3},{2,4},{3,5},{4,6},{5,7},{6,0},{7,1},{8,10},{9,11},{10,... | collective-permute-start | bytes 786440 | tf_op jit(solution)/shard_map/ppermute | solution.py:438
  82.6 11.1 %collective-permute-start.20 = (bf16[256,512]{1,0:T(8,128)(2,1)S(1)}, bf16[256,512]{1,0:T(8,128)(2,1)S(1)}, u32[]{:S(2)}, u32[]{:S(2)}) collective-permute-start(bf16[256,512]{1,0:T(8,128)(2,1)S(1)} %get-tuple-element.89), channel_id=1, source_target_pairs={{0,6},{1,7},{2,0},{3,1},{4,2},{5,3},{6,4},{7,5},{8,14},{9,15},{10,... | collective-permute-start | bytes 786440 | tf_op jit(solution)/shard_map/ppermute | solution.py:439
  (10 other events, 30.7 us)
